TPU v7x, 32 devices: a whole 2x2x4 slice. The times are simulated.
32 devices in a mesh: dp: 16 (over z, x, core), mp: 2 (over y).
Axes of the slice: x: 2, y: 2, z: 4, core: 2. Of those that a mesh axis runs over, the one named last changes fastest.
Arguments:
- inputs: bfloat16 [256, 6144], P('dp', 'mp'), may hold values from -6 to 6
- targets: bfloat16 [256, 6144], P('dp', 'mp'), may hold values from -6 to 6
- w_in: bfloat16 [6144, 16384], P('mp', 'dp'), may hold values from -6 to 6
- w_out: bfloat16 [16384, 6144], P('dp', 'mp'), may hold values from -6 to 6
- teach_in: float32 [6144, 16384], P('mp', 'dp'), may hold values from -6 to 6
- teach_out: float32 [16384, 6144], P('dp', 'mp'), may hold values from -6 to 6
Outputs:
- grad_in: bfloat16 [6144, 16384], P('mp', 'dp')
- grad_out: bfloat16 [16384, 6144], P('dp', 'mp')
- new_in: float32 [6144, 16384], P('mp', 'dp')
- new_out: float32 [16384, 6144], P('dp', 'mp')
All inputs are finite; a program needn't handle non-finite values.
Results may differ from a plain program's by a relative error of at most 0.017.
Values may be sent and summed in bfloat16 or wider, within the bound.
A program may use at most 192 MiB of HBM per device.

v0:
```python
import math

import jax
import jax.numpy as jnp
from jax import lax
from jax.sharding import PartitionSpec as P

D = 6144
FF = 16384


decay_rate = 0.99
step_size = 0.5


def gelu_value(value):
    return 0.5 * value * (1.0 + jax.scipy.special.erf(value * (1.0 / math.sqrt(2.0))))


def gelu_slope(value):
    normal_cdf = 0.5 * (1.0 + jax.scipy.special.erf(value * (1.0 / math.sqrt(2.0))))
    return normal_cdf + value * jnp.exp(-0.5 * value * value) * (1.0 / math.sqrt(2.0 * math.pi))


def shards(inputs, targets, w_in, w_out, teach_in, teach_out):
    in_scale = 1.0 / math.sqrt(D)
    out_scale = 1.0 / math.sqrt(FF)
    gathered = lax.all_gather(inputs, "dp", axis=0, tiled=True)
    partial_pre = jnp.dot(gathered, w_in, preferred_element_type=jnp.float32) * in_scale
    preact = lax.psum(partial_pre, "mp")
    hidden = gelu_value(preact).astype(jnp.bfloat16)
    block = hidden
    summed_rows = lax.psum_scatter(
        jnp.dot(block, w_out, preferred_element_type=jnp.float32) * out_scale,
        "dp",
        scatter_dimension=0,
        tiled=True,
    )
    slope = (inputs.astype(jnp.float32) + summed_rows - targets.astype(jnp.float32)).astype(
        jnp.bfloat16
    )
    piece = lax.all_gather(slope, "dp", axis=0, tiled=True)
    block = hidden
    grad_acc = jnp.einsum("tf,td->fd", block, piece, preferred_element_type=jnp.float32) * out_scale
    slope_part = (
        jnp.einsum("td,fd->tf", piece, w_out, preferred_element_type=jnp.float32) * out_scale
    )
    hidden_slope = lax.psum(slope_part.astype(jnp.bfloat16), "mp").astype(jnp.float32)
    pre_slope = (hidden_slope * gelu_slope(preact)).astype(jnp.bfloat16)
    grad_in = (
        jnp.einsum("td,tf->df", gathered, pre_slope, preferred_element_type=jnp.float32) * in_scale
    )
    new_in = decay_rate * teach_in + (1.0 - decay_rate) * (
        w_in.astype(jnp.float32) - step_size * grad_in
    )
    new_out = decay_rate * teach_out + (1.0 - decay_rate) * (
        w_out.astype(jnp.float32) - step_size * grad_acc
    )
    return (grad_in.astype(jnp.bfloat16), grad_acc.astype(jnp.bfloat16), new_in, new_out)


def solution(mesh):
    return jax.shard_map(
        shards,
        mesh=mesh,
        in_specs=(
            P("dp", "mp"),
            P("dp", "mp"),
            P("mp", "dp"),
            P("dp", "mp"),
            P("mp", "dp"),
            P("dp", "mp"),
        ),
        out_specs=(P("mp", "dp"), P("dp", "mp"), P("mp", "dp"), P("dp", "mp")),
        check_vma=False,
    )
```

profile of v0, /device:TPU:0, one launch (start us, length us, event | category | flops | bytes accessed | tf_op | source)
XLA Modules:
  0.0 296.9 jit_solution(11318101744656116763)
XLA Ops:
  7.2 0.0 all-gather.3.cloned.1.call-start
  7.2 0.7 all-gather.3.cloned.1.call-update
  7.9 0.0 all-reduce.3.cloned.1.call-start
  7.9 44.7 %all-gather.3.cloned.1.call-done = bf16[256,3072]{1,0:T(8,128)(2,1)} async-done(((bf16[16,3072]{1,0:T(8,128)(2,1)}), bf16[256,3072]{1,0:T(8,128)(2,1)}) %all-gather.3.cloned.1.call-update) | async-done | bytes 1572880 | tf_op jit(solution)/shard_map/all_gather | solution.py:28
  52.7 6.0 %convolution_multiply_fusion.2 = f32[256,1024]{1,0:T(8,128)} fusion(bf16[256,3072]{1,0:T(8,128)(2,1)} %all-gather.3.cloned.1.call-done, bf16[3072,1024]{1,0:T(8,128)(2,1)} %param.8), kind=kOutput, calls=%fused_computation.10 | convolution fusion | flops 1610874880 | bytes 8912896 | tf_op jit(solution)/shard_map/dot_general | solution.py:29
  58.7 0.0 all-reduce.3.cloned.1.call-update
  58.7 0.0 copy-start.2
  58.8 0.0 copy-start.3
  58.8 0.0 reduce-scatter.2.cloned.1.call-start
  58.8 39.0 %all-reduce.3.cloned.1.call-done = f32[256,1024]{1,0:T(8,128)} async-done(((f32[256,1024]{1,0:T(8,128)}), f32[256,1024]{1,0:T(8,128)}) %all-reduce.3.cloned.1.call-update) | async-done | bytes 1048592 | tf_op jit(solution)/shard_map/psum | solution.py:30
  97.8 6.6 %convolution_multiply_fusion = f32[256,3072]{1,0:T(8,128)} fusion(bf16[1024,3072]{1,0:T(8,128)(2,1)} %param.9, f32[256,1024]{1,0:T(8,128)} %all-reduce.3.cloned.1.call-done), kind=kOutput, calls=%fused_computation.7 | convolution fusion | flops 1612709888 | bytes 10485760 | tf_op jit(solution)/shard_map/dot_general | solution.py:34
  104.5 0.0 reduce-scatter.2.cloned.1.call-update
  104.5 0.0 all-gather.5.cloned.1.call-start
  104.5 66.3 %reduce-scatter.2.cloned.1.call-done = f32[16,3072]{1,0:T(8,128)} async-done(((f32[256,3072]{1,0:T(8,128)}), f32[16,3072]{1,0:T(8,128)}) %reduce-scatter.2.cloned.1.call-update) | async-done | bytes 196624 | tf_op jit(solution)/shard_map/reduce_scatter | solution.py:33
  170.9 0.0 copy-done.2
  170.9 0.0 copy-done.3
  170.9 1.6 subtract_convert_fusion
  172.5 0.0 all-gather.5.cloned.1.call-update
  172.5 0.2 all-reduce.5.cloned.1.call-start
  172.7 8.6 %copy.11 = bf16[3072,1024]{0,1:T(8,128)(2,1)} copy(bf16[3072,1024]{1,0:T(8,128)(2,1)} %param.8) | data formatting | bytes 12582912 | tf_op args[2]
  181.4 12.6 %copy.10 = f32[3072,1024]{0,1:T(8,128)} copy(f32[3072,1024]{1,0:T(8,128)} %param.10) | data formatting | bytes 25165824 | tf_op args[4]
  194.0 0.0 copy-start
  194.0 18.5 %all-gather.5.cloned.1.call-done = bf16[256,3072]{1,0:T(8,128)(2,1)} async-done(((bf16[16,3072]{1,0:T(8,128)(2,1)}), bf16[256,3072]{1,0:T(8,128)(2,1)}) %all-gather.5.cloned.1.call-update) | async-done | bytes 1572880 | tf_op jit(solution)/shard_map/all_gather | solution.py:42
  212.5 5.9 %fusion.3 = bf16[256,1024]{1,0:T(8,128)(2,1)} fusion(bf16[256,3072]{1,0:T(8,128)(2,1)} %all-gather.5.cloned.1.call-done, bf16[1024,3072]{1,0:T(8,128)(2,1)} %param.9), kind=kOutput, calls=%fused_computation.11 | convolution fusion | flops 1611137024 | bytes 8388608 | tf_op jit(solution)/shard_map/td,fd->tf/dot_general | solution.py:46
  218.4 0.0 all-reduce.5.cloned.1.call-update
  218.4 0.0 copy-done
  218.4 0.0 copy-start.1
  218.4 13.0 %multiply_add_fusion = (f32[1024,3072]{1,0:T(8,128)}, bf16[1024,3072]{1,0:T(8,128)(2,1)}) fusion(bf16[1024,3072]{1,0:T(8,128)(2,1)} %param.9, f32[1024,3072]{1,0:T(8,128)} %param.11, bf16[256,3072]{1,0:T(8,128)(2,1)} %all-gather.5.cloned.1.call-done, f32[256,1024]{1,0:T(8,128)S(1)} %copy-done), kind=kOutput, calls=%fused_computation.3 | convolution fusion | flops 1637089280 | bytes 40370176 | tf_op jit(solution)/shard_map/tf,td->fd/dot_general | solution.py:44
  231.5 14.6 %all-reduce.5.cloned.1.call-done = bf16[256,1024]{1,0:T(8,128)(2,1)} async-done(((bf16[256,1024]{1,0:T(8,128)(2,1)}), bf16[256,1024]{1,0:T(8,128)(2,1)}) %all-reduce.5.cloned.1.call-update) | async-done | bytes 524304 | tf_op jit(solution)/shard_map/psum | solution.py:48
  246.1 0.0 copy-done.1
  246.1 14.2 %fusion.1 = (f32[3072,1024]{0,1:T(8,128)}, f32[1024,3072]{1,0:T(8,128)}) fusion(bf16[3072,1024]{0,1:T(8,128)(2,1)} %copy.11, f32[3072,1024]{0,1:T(8,128)} %copy.10, bf16[256,3072]{1,0:T(8,128)(2,1)S(1)} %copy-done.1, f32[256,1024]{1,0:T(8,128)S(1)} %copy-done, bf16[256,1024]{1,0:T(8,128)(2,1)} %all-reduce.5.cloned.1.call-done), kind=kOutput, calls=%fused_computation.2 | convolution fusion | flops 1632370688 | bytes 47185920 | tf_op jit(solution)/shard_map/td,tf->df/dot_general | solution.py:51
  260.3 12.6 %copy.13 = f32[3072,1024]{1,0:T(8,128)} copy(f32[3072,1024]{0,1:T(8,128)} %get-tuple-element.10) | data formatting | bytes 25165824
  272.9 8.9 %fusion.2 = bf16[3072,1024]{0,1:T(8,128)(2,1)} fusion(f32[1024,3072]{1,0:T(8,128)} %get-tuple-element.11), kind=kLoop, calls=%fused_computation.6 | loop fusion | flops 6291456 | bytes 18874368 | tf_op jit(solution)/shard_map/convert_element_type | solution.py:59
  281.8 8.6 %copy.12 = bf16[3072,1024]{1,0:T(8,128)(2,1)} copy(bf16[3072,1024]{0,1:T(8,128)(2,1)} %fusion.2) | data formatting | bytes 12582912
Async XLA Ops:
  7.2 45.5 %all-gather.3.cloned.1.call-start = ((), (), s32[]{:S(2)}) async-start(), calls=%async_computation.1 | async-start | bytes 1671168 | tf_op jit(solution)/shard_map/all_gather | solution.py:28
  7.9 89.9 %all-reduce.3.cloned.1.call-start = ((), (), s32[]{:S(2)}) async-start(), calls=%async_computation.2 | async-start | bytes 2097152 | tf_op jit(solution)/shard_map/psum | solution.py:30
  58.7 112.1 %copy-start.2 = (bf16[16,3072]{1,0:T(8,128)(2,1)S(1)}, bf16[16,3072]{1,0:T(8,128)(2,1)}, u32[]{:S(2)}) copy-start(bf16[16,3072]{1,0:T(8,128)(2,1)} %param.6) | copy-start | bytes 294916
  58.8 112.1 %copy-start.3 = (bf16[16,3072]{1,0:T(8,128)(2,1)S(1)}, bf16[16,3072]{1,0:T(8,128)(2,1)}, u32[]{:S(2)}) copy-start(bf16[16,3072]{1,0:T(8,128)(2,1)} %param.7) | copy-start | bytes 294916
  58.8 112.1 %reduce-scatter.2.cloned.1.call-start = ((), (), s32[]{:S(2)}) async-start(), calls=%async_computation.3 | async-start | bytes 3342336 | tf_op jit(solution)/shard_map/reduce_scatter | solution.py:33
  104.5 108.0 %all-gather.5.cloned.1.call-start = ((), (), s32[]{:S(2)}) async-start(), calls=%async_computation.4 | async-start | bytes 1671168 | tf_op jit(solution)/shard_map/all_gather | solution.py:42
  172.5 73.6 %all-reduce.5.cloned.1.call-start = ((), (), s32[]{:S(2)}) async-start(), calls=%async_computation.5 | async-start | bytes 1048576 | tf_op jit(solution)/shard_map/psum | solution.py:48
  194.0 24.4 %copy-start = (f32[256,1024]{1,0:T(8,128)S(1)}, f32[256,1024]{1,0:T(8,128)}, u32[]{:S(2)}) copy-start(f32[256,1024]{1,0:T(8,128)} %all-reduce.3.cloned.1.call-done) | copy-start | bytes 3145732
  218.4 27.7 %copy-start.1 = (bf16[256,3072]{1,0:T(8,128)(2,1)S(1)}, bf16[256,3072]{1,0:T(8,128)(2,1)}, u32[]{:S(2)}) copy-start(bf16[256,3072]{1,0:T(8,128)(2,1)} %all-gather.3.cloned.1.call-done) | copy-start | bytes 4718596
Sparse Core Ops, SparseCore 0:
  10.3 42.3 all-gather.2
  58.9 38.9 all-reduce.2
  104.6 66.2 reduce-scatter.1
  173.8 38.6 all-gather.4
  218.5 27.4 all-reduce.4
where the time goes:
time: 298 us; the launch traced here: 297 us
  waiting for transfers between devices  184 us (62%)
  matrix products  45.8 us (15%)
  local copies, waits for them, and re-layouts  42.5 us (14%)
  between operations  13.8 us (5%)
  other arithmetic  10.5 us (4%)
    reduce_scatter x1, waiting for transfers between devices, shards(): lax.psum_scatter(jnp.dot(block, w_out, preferred_element_type=jnp.float32...  66.3 us
    all_gather x1, waiting for transfers between devices, shards(): gathered = lax.all_gather(inputs, 'dp', axis=0, tiled=True)  44.7 us
    unnamed x12, local copies, waits for them, and re-layouts  42.5 us
    psum x1, waiting for transfers between devices, shards(): preact = lax.psum(partial_pre, 'mp')  39 us
    all_gather x1, waiting for transfers between devices, shards(): piece = lax.all_gather(slope, 'dp', axis=0, tiled=True)  18.5 us
    psum x1, waiting for transfers between devices, shards(): lax.psum(slope_part.astype(jnp.bfloat16), 'mp').astype(jnp.float32)  14.6 us
    dot_general x1, matrix products, shards(): jnp.einsum('td,tf->df', gathered, pre_slope, preferred_element_type=jnp.f...  14.2 us
    dot_general x1, matrix products, shards(): jnp.einsum('tf,td->fd', block, piece, preferred_element_type=jnp.float32)  13 us
  transfers between devices with their start and end apart: 5, of which 5 were waited for; matrix products, arithmetic and copies ran while one was open for 12% of the time, Pallas kernels for 0%

commit v1 on v0

v1 whole, which is shorter than its diff:
```python
import functools
import math

import jax
import jax.numpy as jnp
from jax import lax
from jax.experimental import pallas as pl
from jax.experimental.pallas import tpu as pltpu
from jax.sharding import PartitionSpec as P

decay_rate = 0.99
step_size = 0.5
MESH = pl.DeviceIdType.MESH
F32 = jnp.float32
BF16 = jnp.bfloat16
MIB = 1024 * 1024


def normal_cdf(value):
    return 0.5 * (1.0 + lax.erf(value * (1.0 / math.sqrt(2.0))))


def gelu_slope(value, cdf):
    return cdf + value * jnp.exp(-0.5 * value * value) * (1.0 / math.sqrt(2.0 * math.pi))


def forward_kernel(
    nz, in_scale, out_scale,
    x_ref, t_ref, w_in_hbm, w_out_hbm,
    g_hbm, h_hbm, s_hbm, part_hbm, gs_hbm,
    w_in, w_out, g, s, pre_send, pre_recv, pre, h, part, acc, own,
    c_out, c_in, x_out, x_in, z_out, z_in,
    w_sem, o_sem,
    ag_recv, ag_zs, ag_xs, ag_cs,
    sg_recv, sg_zs, sg_xs, sg_cs,
    y_s, y_r, c_s, c_r, x_s, x_r, z_s, z_r,
):
    rows, feats = x_ref.shape
    ff = w_in.shape[1]
    group = 4 * rows
    chunk = 2 * group
    me = lax.axis_index("dp")
    my = lax.axis_index("mp")
    z, xc = me // 4, me % 4
    x, c = xc // 2, xc % 2
    ox, oc = 1 - x, 1 - c

    def index(zi, xi, ci):
        return (zi * 2 + xi) * 2 + ci

    def z_of(k):
        return ((z // 2 + k // 2) % (nz // 2)) * 2 + (z % 2 + k % 2) % 2

    loads = [
        pltpu.make_async_copy(w_in_hbm, w_in, w_sem.at[0]),
        pltpu.make_async_copy(w_out_hbm, w_out, w_sem.at[1]),
    ]
    for load in loads:
        load.start()

    barrier = pltpu.get_barrier_semaphore()
    for k in range(1, nz):
        pl.semaphore_signal(barrier, inc=1, device_id={"dp": index(z_of(k), x, c)}, device_id_type=MESH)
    pl.semaphore_signal(barrier, inc=1, device_id={"dp": index(z, ox, c)}, device_id_type=MESH)
    pl.semaphore_signal(barrier, inc=1, device_id={"dp": index(z, x, oc)}, device_id_type=MESH)
    pl.semaphore_signal(barrier, inc=1, device_id={"mp": 1 - my}, device_id_type=MESH)
    pl.semaphore_wait(barrier, nz + 2)

    def send(src, dst, ssem, rsem, to):
        copy = pltpu.make_async_remote_copy(
            src_ref=src, dst_ref=dst, send_sem=ssem, recv_sem=rsem,
            device_id=to, device_id_type=MESH,
        )
        return copy

    pending = []

    def go(copy):
        copy.start()
        pending.append(copy)

    def gather(buf, recv, zs, xs, cs):
        def shard(o):
            return buf.at[pl.ds(pl.multiple_of(o * rows, rows), rows), :]

        def move(o, ssem, to):
            return send(shard(o), shard(o), ssem, recv.at[o], {"dp": to})

        to_x, to_c = index(z, ox, c), index(z, x, oc)

        def begin():
            go(move(me, xs.at[0], to_x))
            for k in range(1, nz):
                go(move(me, zs.at[k], index(z_of(k), x, c)))
            go(move(me, cs.at[0], to_c))

        def z_arrive(k):
            o = index(z_of(k), x, c)
            move(o, zs.at[k], to_c).wait_recv()
            go(move(o, xs.at[k], to_x))
            go(move(o, cs.at[k], to_c))

        def x_arrive(k):
            o = index(z_of(k), ox, c)
            move(o, xs.at[k], to_c).wait_recv()
            go(move(o, cs.at[nz + k], to_c))

        def c_arrive(k):
            for xi in (x, ox):
                move(index(z_of(k), xi, oc), cs.at[k], to_c).wait_recv()

        def arrive(j):
            if j == 0:
                z_arrive(1)
                x_arrive(0)
                x_arrive(1)
                for k in range(2, nz):
                    z_arrive(k)
            else:
                x_arrive(2 * j)
                x_arrive(2 * j + 1)
            c_arrive(2 * j)
            c_arrive(2 * j + 1)

        return begin, arrive

    def chunk_rows(j):
        return pl.ds(pl.multiple_of((z_of(2 * j) // 2) * chunk, chunk), chunk)

    begin, arrive = gather(g, ag_recv, ag_zs, ag_xs, ag_cs)
    g[pl.ds(pl.multiple_of(me * rows, rows), rows), :] = x_ref[...]
    begin()

    def pre_step(j):
        arrive(j)
        if j == 0:
            loads[0].wait()
        at = chunk_rows(j)
        tile = 256

        @pl.loop(0, ff // tile)
        def _(i):
            cols = pl.ds(pl.multiple_of(i * tile, tile), tile)
            value = jnp.dot(g[at, :], w_in[:, cols], preferred_element_type=F32) * in_scale
            pre[at, cols] = value
            pre_send[at, cols] = value.astype(BF16)

        go(send(pre_send.at[at, :], pre_recv.at[at, :], y_s.at[j], y_r.at[j], {"mp": 1 - my}))

    def out_step(j):
        at = chunk_rows(j)
        send(pre_send.at[at, :], pre_recv.at[at, :], y_s.at[j], y_r.at[j], {"mp": 1 - my}).wait_recv()
        tile = 256

        @pl.loop(0, ff // tile)
        def _(i):
            cols = pl.ds(pl.multiple_of(i * tile, tile), tile)
            value = pre[at, cols] + pre_recv[at, cols].astype(F32)
            cdf = normal_cdf(value)
            h[at, cols] = (value * cdf).astype(BF16)
            pre[at, cols] = gelu_slope(value, cdf)

        if j == 0:
            loads[1].wait()

        @pl.loop(0, feats // tile)
        def _(i):
            cols = pl.ds(pl.multiple_of(i * tile, tile), tile)
            acc[at, cols] = jnp.dot(h[at, :], w_out[:, cols], preferred_element_type=F32) * out_scale

        for k in (2 * j, 2 * j + 1):
            for xi in range(2):
                src = pl.ds(pl.multiple_of(index(z_of(k), xi, oc) * rows, rows), rows)
                c_out[k, pl.ds(xi * rows, rows), :] = acc[src, :].astype(BF16)
            go(send(c_out.at[k], c_in.at[k], c_s.at[k], c_r.at[k], {"dp": index(z, x, oc)}))

    def core_step(k):
        send(c_out.at[k], c_in.at[k], c_s.at[k], c_r.at[k], {"dp": index(z, x, oc)}).wait_recv()

        def total(xi):
            src = pl.ds(pl.multiple_of(index(z_of(k), xi, c) * rows, rows), rows)
            return acc[src, :] + c_in[k, pl.ds(pl.multiple_of(xi * rows, rows), rows), :].astype(F32)

        x_out[k] = total(ox).astype(BF16)
        go(send(x_out.at[k], x_in.at[k], x_s.at[k], x_r.at[k], {"dp": index(z, ox, c)}))
        own[k] = total(x)

    def x_step(k):
        send(x_out.at[k], x_in.at[k], x_s.at[k], x_r.at[k], {"dp": index(z, ox, c)}).wait_recv()
        value = own[k] + x_in[k].astype(F32)
        if k == 0:
            own[k] = value
        else:
            z_out[k] = value.astype(BF16)
            go(send(z_out.at[k], z_in.at[z], z_s.at[k], z_r.at[z], {"dp": index(z_of(k), x, c)}))

    outs = []

    def store(src, dst, i):
        copy = pltpu.make_async_copy(src, dst, o_sem.at[i])
        copy.start()
        outs.append(copy)

    chunks = nz // 2
    for j in range(chunks):
        pre_step(j)
    store(g, g_hbm, 0)
    for j in range(chunks):
        out_step(j)
        if j > 0:
            x_step(2 * j - 2)
            x_step(2 * j - 1)
        core_step(2 * j)
        core_step(2 * j + 1)
    x_step(nz - 2)
    x_step(nz - 1)
    store(h, h_hbm, 1)
    store(pre, gs_hbm, 2)

    begin, arrive = gather(s, sg_recv, sg_zs, sg_xs, sg_cs)
    summed = own[0]
    for k in range(1, nz):
        zi = z_of(k)
        send(z_out.at[k], z_in.at[zi], z_s.at[k], z_r.at[zi], {"dp": index(zi, x, c)}).wait_recv()
        summed += z_in[zi].astype(F32)
    slope = x_ref[...].astype(F32) + summed - t_ref[...].astype(F32)
    s[pl.ds(pl.multiple_of(me * rows, rows), rows), :] = slope.astype(BF16)
    begin()

    for j in range(chunks):
        arrive(j)
        at = chunk_rows(j)
        tile = 256

        @pl.loop(0, ff // tile)
        def _(i):
            units = pl.ds(pl.multiple_of(i * tile, tile), tile)
            value = lax.dot_general(
                s[at, :], w_out[units, :], (((1,), (1,)), ((), ())), preferred_element_type=F32
            )
            part[at, units] = (value * out_scale).astype(BF16)

    store(s, s_hbm, 3)
    store(part, part_hbm, 4)
    for copy in pending:
        copy.wait_send()
    for copy in outs:
        copy.wait()


def forward(nz, in_scale, out_scale, inputs, targets, w_in, w_out):
    rows, feats = inputs.shape
    ff = w_in.shape[1]
    tokens = rows * nz * 4
    dma = pltpu.SemaphoreType.DMA
    vmem = pl.BlockSpec(memory_space=pltpu.VMEM)
    anywhere = pl.BlockSpec(memory_space=pl.ANY)
    return pl.pallas_call(
        functools.partial(forward_kernel, nz, in_scale, out_scale),
        out_shape=(
            jax.ShapeDtypeStruct((tokens, feats), BF16),
            jax.ShapeDtypeStruct((tokens, ff), BF16),
            jax.ShapeDtypeStruct((tokens, feats), BF16),
            jax.ShapeDtypeStruct((tokens, ff), BF16),
            jax.ShapeDtypeStruct((tokens, ff), F32),
        ),
        in_specs=[vmem, vmem, anywhere, anywhere],
        out_specs=(anywhere,) * 5,
        scratch_shapes=[
            pltpu.VMEM((feats, ff), BF16),
            pltpu.VMEM((ff, feats), BF16),
            pltpu.VMEM((tokens, feats), BF16),
            pltpu.VMEM((tokens, feats), BF16),
            pltpu.VMEM((tokens, ff), BF16),
            pltpu.VMEM((tokens, ff), BF16),
            pltpu.VMEM((tokens, ff), F32),
            pltpu.VMEM((tokens, ff), BF16),
            pltpu.VMEM((tokens, ff), BF16),
            pltpu.VMEM((tokens, feats), F32),
            pltpu.VMEM((nz, rows, feats), F32),
            pltpu.VMEM((nz, 2 * rows, feats), BF16),
            pltpu.VMEM((nz, 2 * rows, feats), BF16),
            pltpu.VMEM((nz, rows, feats), BF16),
            pltpu.VMEM((nz, rows, feats), BF16),
            pltpu.VMEM((nz, rows, feats), BF16),
            pltpu.VMEM((nz, rows, feats), BF16),
            dma((2,)), dma((5,)),
            dma((4 * nz,)), dma((nz,)), dma((nz,)), dma((2 * nz,)),
            dma((4 * nz,)), dma((nz,)), dma((nz,)), dma((2 * nz,)),
            dma((nz // 2,)), dma((nz // 2,)),
            dma((nz,)), dma((nz,)), dma((nz,)), dma((nz,)), dma((nz,)), dma((nz,)),
        ],
        compiler_params=pltpu.CompilerParams(
            collective_id=0, has_side_effects=True, vmem_limit_bytes=48 * MIB
        ),
        cost_estimate=pl.CostEstimate(
            flops=6 * tokens * feats * ff, bytes_accessed=6 * feats * ff, transcendentals=0
        ),
        name="forward",
    )(inputs, targets, w_in, w_out)


def blended(teach, weight, grad):
    return decay_rate * teach + (1.0 - decay_rate) * (weight.astype(F32) - step_size * grad)


def out_kernel(scale, h_ref, s_ref, w_ref, t_ref, grad_ref, new_ref):
    grad = lax.dot_general(
        h_ref[...], s_ref[...], (((0,), (0,)), ((), ())), preferred_element_type=F32
    ) * scale
    grad_ref[...] = grad.astype(BF16)
    new_ref[...] = blended(t_ref[...], w_ref[...], grad)


def update_out(scale, hidden, slope, w_out, teach_out):
    ff, feats = w_out.shape
    tokens = hidden.shape[0]
    tile = 128
    row_block = pl.BlockSpec((tile, feats), lambda i: (i, 0))
    return pl.pallas_call(
        functools.partial(out_kernel, scale),
        grid=(ff // tile,),
        out_shape=(jax.ShapeDtypeStruct((ff, feats), BF16), jax.ShapeDtypeStruct((ff, feats), F32)),
        in_specs=[
            pl.BlockSpec((tokens, tile), lambda i: (0, i)),
            pl.BlockSpec((tokens, feats), lambda i: (0, 0)),
            row_block,
            row_block,
        ],
        out_specs=(row_block, row_block),
        compiler_params=pltpu.CompilerParams(vmem_limit_bytes=40 * MIB),
        cost_estimate=pl.CostEstimate(
            flops=2 * tokens * feats * ff, bytes_accessed=12 * feats * ff, transcendentals=0
        ),
        name="update_out",
    )(hidden, slope, w_out, teach_out)


def in_kernel(scale, g_ref, part_ref, other_ref, gs_ref, w_ref, t_ref, grad_ref, new_ref, pre_slope):
    @pl.when(pl.program_id(0) == 0)
    def _():
        total = part_ref[...].astype(F32) + other_ref[...].astype(F32)
        pre_slope[...] = (total * gs_ref[...]).astype(BF16)

    grad = lax.dot_general(
        g_ref[...], pre_slope[...], (((0,), (0,)), ((), ())), preferred_element_type=F32
    ) * scale
    grad_ref[...] = grad.astype(BF16)
    new_ref[...] = blended(t_ref[...], w_ref[...], grad)


def update_in(scale, gathered, part, other, gs, w_in, teach_in):
    feats, ff = w_in.shape
    tokens = gathered.shape[0]
    tile = 384 if feats % 384 == 0 else 128
    row_block = pl.BlockSpec((tile, ff), lambda i: (i, 0))
    whole = pl.BlockSpec((tokens, ff), lambda i: (0, 0))
    return pl.pallas_call(
        functools.partial(in_kernel, scale),
        grid=(feats // tile,),
        out_shape=(jax.ShapeDtypeStruct((feats, ff), BF16), jax.ShapeDtypeStruct((feats, ff), F32)),
        in_specs=[
            pl.BlockSpec((tokens, tile), lambda i: (0, i)),
            whole, whole, whole,
            row_block,
            row_block,
        ],
        out_specs=(row_block, row_block),
        scratch_shapes=[pltpu.VMEM((tokens, ff), BF16)],
        compiler_params=pltpu.CompilerParams(vmem_limit_bytes=40 * MIB),
        cost_estimate=pl.CostEstimate(
            flops=2 * tokens * feats * ff, bytes_accessed=12 * feats * ff, transcendentals=0
        ),
        name="update_in",
    )(gathered, part, other, gs, w_in, teach_in)


def shards(dp, mp, inputs, targets, w_in, w_out, teach_in, teach_out):
    in_scale = 1.0 / math.sqrt(inputs.shape[1] * mp)
    out_scale = 1.0 / math.sqrt(w_out.shape[0] * dp)
    gathered, hidden, slope, part, gs = forward(
        dp // 4, in_scale, out_scale, inputs, targets, w_in, w_out
    )
    other = lax.ppermute(part, "mp", [(0, 1), (1, 0)])
    grad_out, new_out = update_out(out_scale, hidden, slope, w_out, teach_out)
    grad_in, new_in = update_in(in_scale, gathered, part, other, gs, w_in, teach_in)
    return grad_in, grad_out, new_in, new_out


def plain_shards(dp, mp, inputs, targets, w_in, w_out, teach_in, teach_out):
    in_scale = 1.0 / math.sqrt(inputs.shape[1] * mp)
    out_scale = 1.0 / math.sqrt(w_out.shape[0] * dp)
    gathered = lax.all_gather(inputs, "dp", axis=0, tiled=True)
    preact = lax.psum(jnp.dot(gathered, w_in, preferred_element_type=F32) * in_scale, "mp")
    cdf = normal_cdf(preact)
    hidden = (preact * cdf).astype(BF16)
    summed = lax.psum_scatter(
        jnp.dot(hidden, w_out, preferred_element_type=F32) * out_scale,
        "dp", scatter_dimension=0, tiled=True,
    )
    own = (inputs.astype(F32) + summed - targets.astype(F32)).astype(BF16)
    slope = lax.all_gather(own, "dp", axis=0, tiled=True)
    part = jnp.einsum("td,fd->tf", slope, w_out, preferred_element_type=F32) * out_scale
    hidden_slope = lax.psum(part.astype(BF16), "mp").astype(F32)
    pre_slope = (hidden_slope * gelu_slope(preact, cdf)).astype(BF16)
    g_out = jnp.einsum("tf,td->fd", hidden, slope, preferred_element_type=F32) * out_scale
    g_in = jnp.einsum("td,tf->df", gathered, pre_slope, preferred_element_type=F32) * in_scale
    new_in = blended(teach_in, w_in, g_in)
    new_out = blended(teach_out, w_out, g_out)
    return g_in.astype(BF16), g_out.astype(BF16), new_in, new_out


def solution(mesh):
    dp, mp = mesh.shape["dp"], mesh.shape["mp"]
    body = shards if mp == 2 and dp == 16 else plain_shards
    return jax.shard_map(
        functools.partial(body, dp, mp),
        mesh=mesh,
        in_specs=(
            P("dp", "mp"),
            P("dp", "mp"),
            P("mp", "dp"),
            P("dp", "mp"),
            P("mp", "dp"),
            P("dp", "mp"),
        ),
        out_specs=(P("mp", "dp"), P("dp", "mp"), P("mp", "dp"), P("dp", "mp")),
        check_vma=False,
    )
```

time: 298 us -> 101 us (0.34)
  waiting for transfers between devices: 184 us -> 0.01 us
  Pallas kernels: 0 us -> 97 us
  matrix products: 45.8 us -> 0 us
  local copies, waits for them, and re-layouts: 42.5 us -> 2.15 us
  between operations: 13.8 us -> 0.68 us
  other arithmetic: 10.5 us -> 0 us
    pallas_call x0 -> x3, Pallas kernels: none -> 97 us  [the longest x1 67.2 us: forward(): pl.pallas_call(functools.partial(forward_kernel, nz, in_scale, out_scale)...]
    reduce_scatter x1 -> x0, waiting for transfers between devices: 66.3 us -> none  [shards(): lax.psum_scatter(jnp.dot(block, w_out, preferred_element_type=jnp.float32...]
    all_gather x2 -> x0, waiting for transfers between devices: 63.2 us -> none  [the longest x1 44.7 us: shards(): gathered = lax.all_gather(inputs, 'dp', axis=0, tiled=True)]
    psum x2 -> x0, waiting for transfers between devices: 53.6 us -> none  [the longest x1 39 us: shards(): preact = lax.psum(partial_pre, 'mp')]
    dot_general x5 -> x0, matrix products: 45.8 us -> none  [the longest x1 14.2 us: shards(): jnp.einsum('td,tf->df', gathered, pre_slope, preferred_element_type=jnp.f...]
    unnamed x12 -> x8, local copies, waits for them, and re-layouts: 42.5 us -> 2.15 us
    convert_element_type x2 -> x0, other arithmetic: 10.5 us -> none  [the longest x1 8.91 us: shards(): grad_in.astype(jnp.bfloat16)]
  transfers between devices with their start and end apart: 5 -> 1, of which waited for: 5 -> 0; matrix products, arithmetic and copies ran while one was open for 12% -> 0% of each run, Pallas kernels for 0% -> 15%
where the time goes in v1:
time: 101 us; the launch traced here: 99.9 us
  Pallas kernels  97 us (96%)
  local copies, waits for them, and re-layouts  2.15 us (2%)
    pallas_call x1, Pallas kernels, forward(): pl.pallas_call(functools.partial(forward_kernel, nz, in_scale, out_scale)...  67.2 us
    pallas_call x1, Pallas kernels, update_out(): pl.pallas_call(functools.partial(out_kernel, scale), grid=(ff // tile,),...  15.3 us
    pallas_call x1, Pallas kernels, update_in(): pl.pallas_call(functools.partial(in_kernel, scale), grid=(feats // tile,)...  14.4 us
    unnamed x8, local copies, waits for them, and re-layouts  2.15 us
  transfers between devices with their start and end apart: 1, of which 0 were waited for; matrix products, arithmetic and copies ran while one was open for 0% of the time, Pallas kernels for 15%

profile of v1, /device:TPU:0, one launch (start us, length us, event | category | flops | bytes accessed | tf_op | source)
XLA Modules:
  0.0 99.9 jit_solution(3581679479444439808)
XLA Ops:
  0.6 0.0 copy-start
  0.6 0.0 copy-start.2
  0.7 1.0 %copy-done.2 = bf16[16,3072]{1,0:T(8,128)(2,1)S(1)} copy-done((bf16[16,3072]{1,0:T(8,128)(2,1)S(1)}, bf16[16,3072]{1,0:T(8,128)(2,1)}, u32[]{:S(2)}) %copy-start.2) | copy-done | bytes 98328
  1.7 0.0 copy-start.3
  1.7 1.1 %copy-done.3 = bf16[16,3072]{1,0:T(8,128)(2,1)S(1)} copy-done((bf16[16,3072]{1,0:T(8,128)(2,1)S(1)}, bf16[16,3072]{1,0:T(8,128)(2,1)}, u32[]{:S(2)}) %copy-start.3) | copy-done | bytes 98328
  2.8 67.2 %forward.1 = (bf16[256,3072]{1,0:T(8,128)(2,1)S(1)}, bf16[256,1024]{1,0:T(8,128)(2,1)S(1)}, bf16[256,3072]{1,0:T(8,128)(2,1)S(1)}, bf16[256,1024]{1,0:T(8,128)(2,1)S(1)}, f32[256,1024]{1,0:T(8,128)S(1)}) custom-call(bf16[16,3072]{1,0:T(8,128)(2,1)S(1)} %copy-done.2, bf16[16,3072]{1,0:T(8,128)(2,1)S(1)} %copy-done.3, bf16[3072,1024]{1,0:T(8,128)(2,1)} %w_ref.2, ...), custom_call_target="tpu_custom_call" | custom-call | flops 4831838208 | bytes 18874368 | tf_op jit(solution)/shard_map/forward/pallas_call | solution.py:258
  70.0 0.1 collective-permute-start
  70.1 0.0 copy-done
  70.1 0.0 copy-start.1
  70.1 15.3 %update_out.1 = (bf16[1024,3072]{1,0:T(8,128)(2,1)}, f32[1024,3072]{1,0:T(8,128)}) custom-call(bf16[256,1024]{1,0:T(8,128)(2,1)S(1)} %get-tuple-element.17.h_ref, bf16[256,3072]{1,0:T(8,128)(2,1)S(1)} %get-tuple-element.18.s_ref, bf16[1024,3072]{1,0:T(8,128)(2,1)S(1)} %copy-done, f32[1024,3072]{1,0:T(8,128)} %t_ref.5), custom_call_target="tpu_custom_call" | custom-call | flops 1610612736 | bytes 37748736 | tf_op jit(solution)/shard_map/update_out/pallas_call | solution.py:320
  85.5 0.0 collective-permute-done.other_ref
  85.5 0.0 copy-done.1
  85.5 14.4 %update_in.1 = (bf16[3072,1024]{1,0:T(8,128)(2,1)}, f32[3072,1024]{1,0:T(8,128)}) custom-call(bf16[256,3072]{1,0:T(8,128)(2,1)S(1)} %get-tuple-element.13.g_ref, bf16[256,1024]{1,0:T(8,128)(2,1)S(1)} %get-tuple-element.14.part_ref, bf16[256,1024]{1,0:T(8,128)(2,1)S(1)} %collective-permute-done.other_ref, f32[256,1024]{1,0:T(8,128)S(1)} %get-tuple-element.15.gs_ref, ...), custom_call_target="tpu_custom_call" | custom-call | flops 1610612736 | bytes 37748736 | tf_op jit(solution)/shard_map/update_in/pallas_call | solution.py:358
Async XLA Ops:
  0.6 69.5 %copy-start = (bf16[1024,3072]{1,0:T(8,128)(2,1)S(1)}, bf16[1024,3072]{1,0:T(8,128)(2,1)}, u32[]{:S(2)}) copy-start(bf16[1024,3072]{1,0:T(8,128)(2,1)} %w_ref.3) | copy-start | bytes 18874372
  0.6 1.0 %copy-start.2 = (bf16[16,3072]{1,0:T(8,128)(2,1)S(1)}, bf16[16,3072]{1,0:T(8,128)(2,1)}, u32[]{:S(2)}) copy-start(bf16[16,3072]{1,0:T(8,128)(2,1)} %x_ref.1) | copy-start | bytes 294916
  1.7 1.1 %copy-start.3 = (bf16[16,3072]{1,0:T(8,128)(2,1)S(1)}, bf16[16,3072]{1,0:T(8,128)(2,1)}, u32[]{:S(2)}) copy-start(bf16[16,3072]{1,0:T(8,128)(2,1)} %t_ref.3) | copy-start | bytes 294916
  70.0 15.5 %collective-permute-start = (bf16[256,1024]{1,0:T(8,128)(2,1)S(1)}, bf16[256,1024]{1,0:T(8,128)(2,1)S(1)}, u32[]{:S(2)}, u32[]{:S(2)}) collective-permute-start(bf16[256,1024]{1,0:T(8,128)(2,1)S(1)} %get-tuple-element.14.part_ref), channel_id=1, source_target_pairs={{0,1},{1,0},{2,3},{3,2},{4,5},{5,4},{6,7},{7,6},{8,9},{9,8},{10,11... | collective-permute-start | bytes 1572872 | tf_op jit(solution)/shard_map/ppermute | solution.py:384
  70.1 15.4 %copy-start.1 = (bf16[3072,1024]{1,0:T(8,128)(2,1)S(1)}, bf16[3072,1024]{1,0:T(8,128)(2,1)}, u32[]{:S(2)}) copy-start(bf16[3072,1024]{1,0:T(8,128)(2,1)} %w_ref.2) | copy-start | bytes 18874372

commit v2 on v1

v2 whole, which is shorter than its diff:
```python
import functools
import math

import jax
import jax.numpy as jnp
from jax import lax
from jax.experimental import pallas as pl
from jax.experimental.pallas import tpu as pltpu
from jax.sharding import PartitionSpec as P

decay_rate = 0.99
step_size = 0.5
MESH = pl.DeviceIdType.MESH
F32 = jnp.float32
BF16 = jnp.bfloat16
MIB = 1024 * 1024


def normal_cdf(value):
    return 0.5 * (1.0 + lax.erf(value * (1.0 / math.sqrt(2.0))))


def gelu_slope(value, cdf):
    return cdf + value * jnp.exp(-0.5 * value * value) * (1.0 / math.sqrt(2.0 * math.pi))


def blended(teach, weight, grad):
    return decay_rate * teach + (1.0 - decay_rate) * (weight.astype(F32) - step_size * grad)


def forward_kernel(
    nz, in_scale, out_scale,
    x_hbm, t_hbm, w_in_hbm, w_out_hbm, teach_out_hbm,
    g, h, s, part, pre, w_in, w_out, teach_out,
    t_own, pre_send, pre_recv, acc, own,
    c_out, c_in, x_out, x_in, z_out, z_in,
    w_sem,
    ag_recv, ag_zs, ag_xs, ag_cs,
    sg_recv, sg_zs, sg_xs, sg_cs,
    y_s, y_r, c_s, c_r, x_s, x_r, z_s, z_r,
):
    rows, feats = t_own.shape
    ff = w_in.shape[1]
    group = 4 * rows
    me = lax.axis_index("dp")
    my = lax.axis_index("mp")
    z, xc = me // 4, me % 4
    x, c = xc // 2, xc % 2
    ox, oc = 1 - x, 1 - c
    mine = pl.ds(pl.multiple_of(me * rows, rows), rows)

    def index(zi, xi, ci):
        return (zi * 2 + xi) * 2 + ci

    def z_of(k):
        return ((z // 2 + k // 2) % (nz // 2)) * 2 + (z % 2 + k % 2) % 2

    loads = [
        pltpu.make_async_copy(src, dst, w_sem.at[i])
        for i, (src, dst) in enumerate((
            (x_hbm, g.at[mine, :]), (t_hbm, t_own), (w_in_hbm, w_in),
            (w_out_hbm, w_out), (teach_out_hbm, teach_out),
        ))
    ]
    for load in loads[:3]:
        load.start()

    barrier = pltpu.get_barrier_semaphore()
    for k in range(1, nz):
        pl.semaphore_signal(barrier, inc=1, device_id={"dp": index(z_of(k), x, c)}, device_id_type=MESH)
    pl.semaphore_signal(barrier, inc=1, device_id={"dp": index(z, ox, c)}, device_id_type=MESH)
    pl.semaphore_signal(barrier, inc=1, device_id={"dp": index(z, x, oc)}, device_id_type=MESH)
    pl.semaphore_signal(barrier, inc=1, device_id={"mp": 1 - my}, device_id_type=MESH)
    pl.semaphore_wait(barrier, nz + 2)

    def send(src, dst, ssem, rsem, to):
        return pltpu.make_async_remote_copy(
            src_ref=src, dst_ref=dst, send_sem=ssem, recv_sem=rsem,
            device_id=to, device_id_type=MESH,
        )

    pending = []

    def go(copy):
        copy.start()
        pending.append(copy)

    def gather(buf, recv, zs, xs, cs):
        def shard(o):
            return buf.at[pl.ds(pl.multiple_of(o * rows, rows), rows), :]

        def move(o, ssem, to):
            return send(shard(o), shard(o), ssem, recv.at[o], {"dp": to})

        to_x, to_c = index(z, ox, c), index(z, x, oc)

        def begin():
            go(move(me, xs.at[0], to_x))
            for k in range(1, nz):
                go(move(me, zs.at[k], index(z_of(k), x, c)))
            go(move(me, cs.at[0], to_c))

        def z_arrive(k):
            o = index(z_of(k), x, c)
            move(o, zs.at[k], to_c).wait_recv()
            go(move(o, xs.at[k], to_x))
            go(move(o, cs.at[k], to_c))

        def x_arrive(k):
            o = index(z_of(k), ox, c)
            move(o, xs.at[k], to_c).wait_recv()
            go(move(o, cs.at[nz + k], to_c))

        def c_arrive(k):
            for xi in (x, ox):
                move(index(z_of(k), xi, oc), cs.at[k], to_c).wait_recv()

        return begin, z_arrive, x_arrive, c_arrive

    def group_rows(k):
        return pl.ds(pl.multiple_of(z_of(k) * group, group), group)

    def pair_rows(j):
        return pl.ds(pl.multiple_of((z_of(2 * j) // 2) * 2 * group, 2 * group), 2 * group)

    begin, z_arrive, x_arrive, c_arrive = gather(g, ag_recv, ag_zs, ag_xs, ag_cs)
    loads[0].wait()
    begin()
    for load in loads[3:]:
        load.start()

    def pre_step(k):
        x_arrive(k)
        c_arrive(k)
        if k == 0:
            loads[2].wait()
        at = group_rows(k)
        tile = 256

        @pl.loop(0, ff // tile)
        def _(i):
            cols = pl.ds(pl.multiple_of(i * tile, tile), tile)
            value = jnp.dot(g[at, :], w_in[:, cols], preferred_element_type=F32) * in_scale
            pre[at, cols] = value
            pre_send[at, cols] = value.astype(BF16)

        go(send(pre_send.at[at, :], pre_recv.at[at, :], y_s.at[k], y_r.at[k], {"mp": 1 - my}))

    def out_step(k):
        at = group_rows(k)
        send(pre_send.at[at, :], pre_recv.at[at, :], y_s.at[k], y_r.at[k], {"mp": 1 - my}).wait_recv()
        tile = 256

        @pl.loop(0, ff // tile)
        def _(i):
            cols = pl.ds(pl.multiple_of(i * tile, tile), tile)
            value = pre[at, cols] + pre_recv[at, cols].astype(F32)
            cdf = normal_cdf(value)
            h[at, cols] = (value * cdf).astype(BF16)
            pre[at, cols] = gelu_slope(value, cdf)

        if k == 0:
            loads[3].wait()

        @pl.loop(0, feats // tile)
        def _(i):
            cols = pl.ds(pl.multiple_of(i * tile, tile), tile)
            acc[at, cols] = jnp.dot(h[at, :], w_out[:, cols], preferred_element_type=F32) * out_scale

        for xi in range(2):
            src = pl.ds(pl.multiple_of(index(z_of(k), xi, oc) * rows, rows), rows)
            c_out[k, pl.ds(xi * rows, rows), :] = acc[src, :].astype(BF16)
        go(send(c_out.at[k], c_in.at[k], c_s.at[k], c_r.at[k], {"dp": index(z, x, oc)}))

    def core_step(k):
        send(c_out.at[k], c_in.at[k], c_s.at[k], c_r.at[k], {"dp": index(z, x, oc)}).wait_recv()

        def total(xi):
            src = pl.ds(pl.multiple_of(index(z_of(k), xi, c) * rows, rows), rows)
            return acc[src, :] + c_in[k, pl.ds(pl.multiple_of(xi * rows, rows), rows), :].astype(F32)

        x_out[k] = total(ox).astype(BF16)
        go(send(x_out.at[k], x_in.at[k], x_s.at[k], x_r.at[k], {"dp": index(z, ox, c)}))
        own[k] = total(x)

    def x_step(k):
        send(x_out.at[k], x_in.at[k], x_s.at[k], x_r.at[k], {"dp": index(z, ox, c)}).wait_recv()
        value = own[k] + x_in[k].astype(F32)
        if k == 0:
            own[k] = value
        else:
            z_out[k] = value.astype(BF16)
            go(send(z_out.at[k], z_in.at[z], z_s.at[k], z_r.at[z], {"dp": index(z_of(k), x, c)}))

    z_arrive(1)
    pre_step(0)
    pre_step(1)
    for k in range(2, nz):
        z_arrive(k)
    for k in range(nz):
        out_step(k)
        if k + 2 < nz:
            pre_step(k + 2)
        if k > 0:
            x_step(k - 1)
        core_step(k)
    x_step(nz - 1)

    begin, z_arrive, x_arrive, c_arrive = gather(s, sg_recv, sg_zs, sg_xs, sg_cs)
    loads[1].wait()
    summed = own[0]
    for k in range(1, nz):
        zi = z_of(k)
        send(z_out.at[k], z_in.at[zi], z_s.at[k], z_r.at[zi], {"dp": index(zi, x, c)}).wait_recv()
        summed += z_in[zi].astype(F32)
    slope = g[mine, :].astype(F32) + summed - t_own[...].astype(F32)
    s[mine, :] = slope.astype(BF16)
    begin()

    for j in range(nz // 2):
        if j == 0:
            z_arrive(1)
            x_arrive(0)
            x_arrive(1)
            for k in range(2, nz):
                z_arrive(k)
        else:
            x_arrive(2 * j)
            x_arrive(2 * j + 1)
        c_arrive(2 * j)
        c_arrive(2 * j + 1)
        at = pair_rows(j)
        tile = 256

        @pl.loop(0, ff // tile)
        def _(i):
            units = pl.ds(pl.multiple_of(i * tile, tile), tile)
            value = lax.dot_general(
                s[at, :], w_out[units, :], (((1,), (1,)), ((), ())), preferred_element_type=F32
            )
            part[at, units] = (value * out_scale).astype(BF16)

    for copy in pending:
        copy.wait_send()
    for load in loads[4:]:
        load.wait()


def forward(nz, in_scale, out_scale, inputs, targets, w_in, w_out, teach_out):
    rows, feats = inputs.shape
    ff = w_in.shape[1]
    tokens = rows * nz * 4
    dma = pltpu.SemaphoreType.DMA
    vmem = pl.BlockSpec(memory_space=pltpu.VMEM)
    return pl.pallas_call(
        functools.partial(forward_kernel, nz, in_scale, out_scale),
        out_shape=(
            pltpu.VMEM((tokens, feats), BF16),
            pltpu.VMEM((tokens, ff), BF16),
            pltpu.VMEM((tokens, feats), BF16),
            pltpu.VMEM((tokens, ff), BF16),
            pltpu.VMEM((tokens, ff), F32),
            pltpu.VMEM((feats, ff), BF16),
            pltpu.VMEM((ff, feats), BF16),
            pltpu.VMEM((ff, feats), F32),
        ),
        in_specs=[pl.BlockSpec(memory_space=pltpu.HBM)] * 5,
        out_specs=(vmem,) * 8,
        scratch_shapes=[
            pltpu.VMEM((rows, feats), BF16),
            pltpu.VMEM((tokens, ff), BF16),
            pltpu.VMEM((tokens, ff), BF16),
            pltpu.VMEM((tokens, feats), F32),
            pltpu.VMEM((nz, rows, feats), F32),
            pltpu.VMEM((nz, 2 * rows, feats), BF16),
            pltpu.VMEM((nz, 2 * rows, feats), BF16),
            pltpu.VMEM((nz, rows, feats), BF16),
            pltpu.VMEM((nz, rows, feats), BF16),
            pltpu.VMEM((nz, rows, feats), BF16),
            pltpu.VMEM((nz, rows, feats), BF16),
            dma((5,)),
            dma((4 * nz,)), dma((nz,)), dma((nz,)), dma((2 * nz,)),
            dma((4 * nz,)), dma((nz,)), dma((nz,)), dma((2 * nz,)),
            dma((nz,)), dma((nz,)),
            dma((nz,)), dma((nz,)), dma((nz,)), dma((nz,)), dma((nz,)), dma((nz,)),
        ],
        compiler_params=pltpu.CompilerParams(
            collective_id=0, has_side_effects=True, vmem_limit_bytes=12 * MIB
        ),
        cost_estimate=pl.CostEstimate(
            flops=6 * tokens * feats * ff, bytes_accessed=12 * feats * ff, transcendentals=0
        ),
        name="forward",
    )(*[
        pltpu.with_memory_space_constraint(x, pltpu.HBM)
        for x in (inputs, targets, w_in, w_out, teach_out)
    ])


def write_update(scale, tile, cols_tile, left, right, w, t, grad_hbm, new_hbm, grads, news, turned, sems):
    count, width = w.shape
    slots = grads.shape[0]
    copies = []
    for i in range(count // tile):
        slot = i % slots
        if i >= slots:
            for copy in copies[i - slots]:
                copy.wait()
        at = pl.ds(i * tile, tile)
        turned[...] = left[:, i * tile:(i + 1) * tile].T

        @pl.loop(0, width // cols_tile)
        def _(n):
            cols = pl.ds(pl.multiple_of(n * cols_tile, cols_tile), cols_tile)
            grad = jnp.dot(turned[...], right[:, cols], preferred_element_type=F32) * scale
            grads[slot, :, cols] = grad.astype(BF16)
            news[slot, :, cols] = blended(t[at, cols], w[at, cols], grad)

        pair = (
            pltpu.make_async_copy(grads.at[slot], grad_hbm.at[at, :], sems.at[0, slot]),
            pltpu.make_async_copy(news.at[slot], new_hbm.at[at, :], sems.at[1, slot]),
        )
        for copy in pair:
            copy.start()
        copies.append(pair)
    for pair in copies[-slots:]:
        for copy in pair:
            copy.wait()


def out_kernel(scale, tile, cols, h, s, w, t, *rest):
    write_update(scale, tile, cols, h, s, w, t, *rest)


def in_kernel(scale, tile, cols, g, part, other, gs, w, t, grad_hbm, new_hbm, grads, news, turned, sems, pre_slope):
    total = part[...].astype(F32) + other[...].astype(F32)
    pre_slope[...] = (total * gs[...]).astype(BF16)
    write_update(scale, tile, cols, g, pre_slope, w, t, grad_hbm, new_hbm, grads, news, turned, sems)


def update(kernel, name, scale, tile, cols, extra, tokens, *operands):
    count, width = operands[-1].shape
    slots = 3
    vmem = pl.BlockSpec(memory_space=pltpu.VMEM)
    anywhere = pl.BlockSpec(memory_space=pl.ANY)
    return pl.pallas_call(
        functools.partial(kernel, scale, tile, cols),
        out_shape=(
            jax.ShapeDtypeStruct((count, width), BF16),
            jax.ShapeDtypeStruct((count, width), F32),
        ),
        in_specs=[vmem] * len(operands),
        out_specs=(anywhere, anywhere),
        scratch_shapes=[
            pltpu.VMEM((slots, tile, width), BF16),
            pltpu.VMEM((slots, tile, width), F32),
            pltpu.VMEM((tile, tokens), BF16),
            pltpu.SemaphoreType.DMA((2, slots)),
            *extra,
        ],
        compiler_params=pltpu.CompilerParams(vmem_limit_bytes=12 * MIB),
        cost_estimate=pl.CostEstimate(
            flops=2 * tokens * count * width, bytes_accessed=12 * count * width, transcendentals=0
        ),
        name=name,
    )(*[pltpu.with_memory_space_constraint(x, pltpu.VMEM) for x in operands])


def shards(dp, mp, inputs, targets, w_in, w_out, teach_in, teach_out):
    in_scale = 1.0 / math.sqrt(inputs.shape[1] * mp)
    out_scale = 1.0 / math.sqrt(w_out.shape[0] * dp)
    tokens, ff = inputs.shape[0] * dp, w_in.shape[1]
    g, h, s, part, gs, w_in, w_out, teach_out = forward(
        dp // 4, in_scale, out_scale, inputs, targets, w_in, w_out, teach_out
    )
    other = lax.ppermute(part, "mp", [(0, 1), (1, 0)])
    grad_out, new_out = update(
        out_kernel, "update_out", out_scale, 128, 512, (), tokens,
        h, s, w_out, teach_out,
    )
    grad_in, new_in = update(
        in_kernel, "update_in", in_scale, 384, 256, (pltpu.VMEM((tokens, ff), BF16),), tokens,
        g, part, other, gs, w_in, teach_in,
    )
    return grad_in, grad_out, new_in, new_out


def plain_shards(dp, mp, inputs, targets, w_in, w_out, teach_in, teach_out):
    in_scale = 1.0 / math.sqrt(inputs.shape[1] * mp)
    out_scale = 1.0 / math.sqrt(w_out.shape[0] * dp)
    gathered = lax.all_gather(inputs, "dp", axis=0, tiled=True)
    preact = lax.psum(jnp.dot(gathered, w_in, preferred_element_type=F32) * in_scale, "mp")
    cdf = normal_cdf(preact)
    hidden = (preact * cdf).astype(BF16)
    summed = lax.psum_scatter(
        jnp.dot(hidden, w_out, preferred_element_type=F32) * out_scale,
        "dp", scatter_dimension=0, tiled=True,
    )
    own = (inputs.astype(F32) + summed - targets.astype(F32)).astype(BF16)
    slope = lax.all_gather(own, "dp", axis=0, tiled=True)
    part = jnp.einsum("td,fd->tf", slope, w_out, preferred_element_type=F32) * out_scale
    hidden_slope = lax.psum(part.astype(BF16), "mp").astype(F32)
    pre_slope = (hidden_slope * gelu_slope(preact, cdf)).astype(BF16)
    g_out = jnp.einsum("tf,td->fd", hidden, slope, preferred_element_type=F32) * out_scale
    g_in = jnp.einsum("td,tf->df", gathered, pre_slope, preferred_element_type=F32) * in_scale
    new_in = blended(teach_in, w_in, g_in)
    new_out = blended(teach_out, w_out, g_out)
    return g_in.astype(BF16), g_out.astype(BF16), new_in, new_out


def solution(mesh):
    dp, mp = mesh.shape["dp"], mesh.shape["mp"]
    body = shards if mp == 2 and dp == 16 else plain_shards
    return jax.shard_map(
        functools.partial(body, dp, mp),
        mesh=mesh,
        in_specs=(
            P("dp", "mp"),
            P("dp", "mp"),
            P("mp", "dp"),
            P("dp", "mp"),
            P("mp", "dp"),
            P("dp", "mp"),
        ),
        out_specs=(P("mp", "dp"), P("dp", "mp"), P("mp", "dp"), P("dp", "mp")),
        check_vma=False,
    )
```

time: 101 us -> 92.2 us (0.913)
  Pallas kernels: 97 us -> 89.8 us
  local copies, waits for them, and re-layouts: 2.15 us -> 0.02 us
  waiting for transfers between devices: 0.01 us -> 1.47 us
    pallas_call x2, Pallas kernels: 29.7 us -> 24.1 us  [update(): pl.pallas_call(functools.partial(kernel, scale, tile, cols), out_shape=(j...]
    unnamed x8 -> x6, local copies, waits for them, and re-layouts: 2.15 us -> 0.02 us
    pallas_call x1, Pallas kernels: 67.2 us -> 65.6 us  [forward(): pl.pallas_call(functools.partial(forward_kernel, nz, in_scale, out_scale)...]
    ppermute x1, waiting for transfers between devices: 0.01 us -> 1.47 us  [shards(): other = lax.ppermute(part, 'mp', [(0, 1), (1, 0)])]
  transfers between devices with their start and end apart: 1 -> 1, of which waited for: 0 -> 1; matrix products, arithmetic and copies ran while one was open for 0% -> 0% of each run, Pallas kernels for 15% -> 14%
where the time goes in v2:
time: 92.2 us; the launch traced here: 92 us
  Pallas kernels  89.8 us (97%)
  waiting for transfers between devices  1.47 us (2%)
    pallas_call x1, Pallas kernels, forward(): pl.pallas_call(functools.partial(forward_kernel, nz, in_scale, out_scale)...  65.6 us
    pallas_call x2, Pallas kernels, update(): pl.pallas_call(functools.partial(kernel, scale, tile, cols), out_shape=(j...  24.1 us
  transfers between devices with their start and end apart: 1, of which 1 were waited for; matrix products, arithmetic and copies ran while one was open for 0% of the time, Pallas kernels for 14%

profile of v2, /device:TPU:0, one launch (start us, length us, event | category | flops | bytes accessed | tf_op | source)
XLA Modules:
  0.0 92.0 jit_solution(11729622704865462815)
XLA Ops:
  0.6 0.0 slice-start
  0.6 0.0 slice-start.1
  0.7 65.6 %forward.1 = (bf16[256,3072]{1,0:T(8,128)(2,1)S(1)}, bf16[256,1024]{1,0:T(8,128)(2,1)S(1)}, bf16[256,3072]{1,0:T(8,128)(2,1)S(1)}, bf16[256,1024]{1,0:T(8,128)(2...) custom-call(bf16[16,3072]{1,0:T(8,128)(2,1)} %x_hbm.1, ...), custom_call_target="tpu_custom_call" | custom-call | flops 4831838208 | bytes 37748736 | tf_op jit(solution)/shard_map/forward/pallas_call | solution.py:255
  66.3 0.1 collective-permute-start
  66.4 0.0 slice-start.2
  66.4 13.0 %update_out.1 = (bf16[1024,3072]{1,0:T(8,128)(2,1)}, f32[1024,3072]{1,0:T(8,128)}) custom-call(bf16[256,1024]{1,0:T(8,128)(2,1)S(1)} %get-tuple-element.21.h, bf16[256,3072]{1,0:T(8,128)(2,1)S(1)} %get-tuple-element.22.s, bf16[1024,3072]{1,0:T(8,128)(2,1)S(1)} %get-tuple-element.23.w, f32[1024,3072]{1,0:T(8,128)S(1)} %get-tuple-element.24.t), custom_call_target="tpu_custom_call" | custom-call | flops 1610612736 | bytes 37748736 | tf_op jit(solution)/shard_map/update_out/pallas_call | solution.py:346
  79.4 1.5 %collective-permute-done.other = bf16[256,1024]{1,0:T(8,128)(2,1)S(1)} collective-permute-done((bf16[256,1024]{1,0:T(8,128)(2,1)S(1)}, bf16[256,1024]{1,0:T(8,128)(2,1)S(1)}, u32[]{:S(2)}, u32[]{:S(2)}) %collective-permute-start) | collective-permute-done | bytes 524320 | tf_op jit(solution)/shard_map/ppermute | solution.py:376
  80.9 0.0 slice-done
  80.9 0.0 slice-done.1
  80.9 0.0 slice-done.2
  80.9 11.1 %update_in.1 = (bf16[3072,1024]{1,0:T(8,128)(2,1)}, f32[3072,1024]{1,0:T(8,128)}) custom-call(bf16[256,3072]{1,0:T(8,128)(2,1)S(1)} %get-tuple-element.16.g, bf16[256,1024]{1,0:T(8,128)(2,1)S(1)} %get-tuple-element.17.part, bf16[256,1024]{1,0:T(8,128)(2,1)S(1)} %collective-permute-done.other, f32[256,1024]{1,0:T(8,128)S(1)} %get-tuple-element.18.gs, ...), custom_call_target="tpu_custom_call" | custom-call | flops 1610612736 | bytes 37748736 | tf_op jit(solution)/shard_map/update_in/pallas_call | solution.py:346
  (1 shorter events, 0.0 us)
Async XLA Ops:
  0.6 80.2 %slice-start = ((s8[12582912]{0:T(1024)(128)(4,1)}), s8[4194304]{0:T(1024)(128)(4,1)S(1)}, s32[]{:S(2)}) async-start(s8[12582912]{0:T(1024)(128)(4,1)} %bitcast), calls=%async_computation | async-start | bytes 8388608
  0.6 80.2 %slice-start.1 = ((s8[12582912]{0:T(1024)(128)(4,1)}), s8[4194304]{0:T(1024)(128)(4,1)S(1)}, s32[]{:S(2)}) async-start(s8[12582912]{0:T(1024)(128)(4,1)} %bitcast), calls=%async_computation.1 | async-start | bytes 8388608
  66.3 14.6 %collective-permute-start = (bf16[256,1024]{1,0:T(8,128)(2,1)S(1)}, bf16[256,1024]{1,0:T(8,128)(2,1)S(1)}, u32[]{:S(2)}, u32[]{:S(2)}) collective-permute-start(bf16[256,1024]{1,0:T(8,128)(2,1)S(1)} %get-tuple-element.17.part), channel_id=1, source_target_pairs={{0,1},{1,0},{2,3},{3,2},{4,5},{5,4},{6,7},{7,6},{8,9},{9,8},{10,11... | collective-permute-start | bytes 1572872 | tf_op jit(solution)/shard_map/ppermute | solution.py:376
  66.4 14.5 %slice-start.2 = ((s8[12582912]{0:T(1024)(128)(4,1)}), s8[4194304]{0:T(1024)(128)(4,1)S(1)}, s32[]{:S(2)}) async-start(s8[12582912]{0:T(1024)(128)(4,1)} %bitcast), calls=%async_computation.2 | async-start | bytes 8388608

commit v3 on v2

--- a/solution.py
+++ b/solution.py
@@ -120,9 +120,6 @@
     def group_rows(k):
         return pl.ds(pl.multiple_of(z_of(k) * group, group), group)
 
-    def pair_rows(j):
-        return pl.ds(pl.multiple_of((z_of(2 * j) // 2) * 2 * group, 2 * group), 2 * group)
-
     begin, z_arrive, x_arrive, c_arrive = gather(g, ag_recv, ag_zs, ag_xs, ag_cs)
     loads[0].wait()
     begin()
@@ -135,7 +132,7 @@
         if k == 0:
             loads[2].wait()
         at = group_rows(k)
-        tile = 256
+        tile = min(512, ff)
 
         @pl.loop(0, ff // tile)
         def _(i):
@@ -162,9 +159,11 @@
         if k == 0:
             loads[3].wait()
 
-        @pl.loop(0, feats // tile)
+        wide = 1024 if feats % 1024 == 0 else 256
+
+        @pl.loop(0, feats // wide)
         def _(i):
-            cols = pl.ds(pl.multiple_of(i * tile, tile), tile)
+            cols = pl.ds(pl.multiple_of(i * wide, wide), wide)
             acc[at, cols] = jnp.dot(h[at, :], w_out[:, cols], preferred_element_type=F32) * out_scale
 
         for xi in range(2):
@@ -217,28 +216,24 @@
     s[mine, :] = slope.astype(BF16)
     begin()
 
-    for j in range(nz // 2):
-        if j == 0:
-            z_arrive(1)
-            x_arrive(0)
-            x_arrive(1)
-            for k in range(2, nz):
-                z_arrive(k)
-        else:
-            x_arrive(2 * j)
-            x_arrive(2 * j + 1)
-        c_arrive(2 * j)
-        c_arrive(2 * j + 1)
-        at = pair_rows(j)
-        tile = 256
-
-        @pl.loop(0, ff // tile)
-        def _(i):
-            units = pl.ds(pl.multiple_of(i * tile, tile), tile)
-            value = lax.dot_general(
-                s[at, :], w_out[units, :], (((1,), (1,)), ((), ())), preferred_element_type=F32
-            )
-            part[at, units] = (value * out_scale).astype(BF16)
+    z_arrive(1)
+    x_arrive(0)
+    x_arrive(1)
+    for k in range(2, nz):
+        z_arrive(k)
+    for k in range(2, nz):
+        x_arrive(k)
+    for k in range(nz):
+        c_arrive(k)
+    tile = min(512, ff)
+
+    @pl.loop(0, ff // tile)
+    def _(i):
+        units = pl.ds(pl.multiple_of(i * tile, tile), tile)
+        value = lax.dot_general(
+            s[...], w_out[units, :], (((1,), (1,)), ((), ())), preferred_element_type=F32
+        )
+        part[:, units] = (value * out_scale).astype(BF16)
 
     for copy in pending:
         copy.wait_send()
@@ -300,31 +295,36 @@
 def write_update(scale, tile, cols_tile, left, right, w, t, grad_hbm, new_hbm, grads, news, turned, sems):
     count, width = w.shape
     slots = grads.shape[0]
-    copies = []
-    for i in range(count // tile):
+    steps = count // tile
+
+    def writes(i, slot):
+        at = pl.ds(pl.multiple_of(i * tile, tile), tile)
+        return (
+            pltpu.make_async_copy(grads.at[slot], grad_hbm.at[at, :], sems.at[0, slot]),
+            pltpu.make_async_copy(news.at[slot], new_hbm.at[at, :], sems.at[1, slot]),
+        )
+
+    @pl.loop(0, steps)
+    def _(i):
         slot = i % slots
-        if i >= slots:
-            for copy in copies[i - slots]:
+
+        @pl.when(i >= slots)
+        def _():
+            for copy in writes(i - slots, slot):
                 copy.wait()
-        at = pl.ds(i * tile, tile)
-        turned[...] = left[:, i * tile:(i + 1) * tile].T
-
-        @pl.loop(0, width // cols_tile)
-        def _(n):
-            cols = pl.ds(pl.multiple_of(n * cols_tile, cols_tile), cols_tile)
+
+        at = pl.ds(pl.multiple_of(i * tile, tile), tile)
+        turned[...] = left[:, at].T
+        for n in range(0, width, cols_tile):
+            cols = slice(n, n + cols_tile)
             grad = jnp.dot(turned[...], right[:, cols], preferred_element_type=F32) * scale
             grads[slot, :, cols] = grad.astype(BF16)
             news[slot, :, cols] = blended(t[at, cols], w[at, cols], grad)
-
-        pair = (
-            pltpu.make_async_copy(grads.at[slot], grad_hbm.at[at, :], sems.at[0, slot]),
-            pltpu.make_async_copy(news.at[slot], new_hbm.at[at, :], sems.at[1, slot]),
-        )
-        for copy in pair:
+        for copy in writes(i, slot):
             copy.start()
-        copies.append(pair)
-    for pair in copies[-slots:]:
-        for copy in pair:
+
+    for i in range(max(steps - slots, 0), steps):
+        for copy in writes(i, i % slots):
             copy.wait()
 
 
@@ -375,7 +375,7 @@
     )
     other = lax.ppermute(part, "mp", [(0, 1), (1, 0)])
     grad_out, new_out = update(
-        out_kernel, "update_out", out_scale, 128, 512, (), tokens,
+        out_kernel, "update_out", out_scale, 128, 256, (), tokens,
         h, s, w_out, teach_out,
     )
     grad_in, new_in = update(

time: 92.2 us -> 85.9 us (0.932)
  Pallas kernels: 89.8 us -> 76.9 us
  waiting for transfers between devices: 1.47 us -> 5.7 us
  starting transfers between devices: 0.07 us -> 1.58 us
    pallas_call x2, Pallas kernels: 24.1 us -> 14.6 us  [update(): pl.pallas_call(functools.partial(kernel, scale, tile, cols), out_shape=(j...]
    ppermute x1, waiting for transfers between devices: 1.47 us -> 5.7 us  [shards(): other = lax.ppermute(part, 'mp', [(0, 1), (1, 0)])]
    pallas_call x1, Pallas kernels: 65.6 us -> 62.3 us  [forward(): pl.pallas_call(functools.partial(forward_kernel, nz, in_scale, out_scale)...]
    ppermute x1, starting transfers between devices: 0.07 us -> 1.58 us  [shards(): other = lax.ppermute(part, 'mp', [(0, 1), (1, 0)])]
  transfers between devices with their start and end apart: 1 -> 1, of which waited for: 1 -> 1; matrix products, arithmetic and copies ran while one was open for 0% -> 0% of each run, Pallas kernels for 14% -> 9%
where the time goes in v3:
time: 85.9 us; the launch traced here: 84.8 us
  Pallas kernels  76.9 us (90%)
  waiting for transfers between devices  5.7 us (7%)
  starting transfers between devices  1.58 us (2%)
    pallas_call x1, Pallas kernels, forward(): pl.pallas_call(functools.partial(forward_kernel, nz, in_scale, out_scale)...  62.3 us
    pallas_call x2, Pallas kernels, update(): pl.pallas_call(functools.partial(kernel, scale, tile, cols), out_shape=(j...  14.6 us
    ppermute x1, waiting for transfers between devices, shards(): other = lax.ppermute(part, 'mp', [(0, 1), (1, 0)])  5.7 us
  transfers between devices with their start and end apart: 1, of which 1 were waited for; matrix products, arithmetic and copies ran while one was open for 0% of the time, Pallas kernels for 9%

profile of v3, /device:TPU:0, one launch (start us, length us, event | category | flops | bytes accessed | tf_op | source)
XLA Modules:
  0.0 84.8 jit_solution(1361262271239049206)
XLA Ops:
  0.6 0.0 slice-start
  0.6 0.0 slice-start.1
  0.7 62.3 %forward.1 = (bf16[256,3072]{1,0:T(8,128)(2,1)S(1)}, bf16[256,1024]{1,0:T(8,128)(2,1)S(1)}, bf16[256,3072]{1,0:T(8,128)(2,1)S(1)}, bf16[256,1024]{1,0:T(8,128)(2...) custom-call(bf16[16,3072]{1,0:T(8,128)(2,1)} %x_hbm.1, ...), custom_call_target="tpu_custom_call" | custom-call | flops 4831838208 | bytes 37748736 | tf_op jit(solution)/shard_map/forward/pallas_call | solution.py:250
  63.0 1.6 %collective-permute-start = (bf16[256,1024]{1,0:T(8,128)(2,1)S(1)}, bf16[256,1024]{1,0:T(8,128)(2,1)S(1)}, u32[]{:S(2)}, u32[]{:S(2)}) collective-permute-start(bf16[256,1024]{1,0:T(8,128)(2,1)S(1)} %get-tuple-element.17.part), channel_id=1, source_target_pairs={{0,1},{1,0},{2,3},{3,2},{4,5},{5,4},{6,7},{7,6},{8,9},{9,8},{10,11... | collective-permute-start | bytes 1572872 | tf_op jit(solution)/shard_map/ppermute | solution.py:376
  64.6 0.0 slice-start.2
  64.6 7.3 %update_out.1 = (bf16[1024,3072]{1,0:T(8,128)(2,1)}, f32[1024,3072]{1,0:T(8,128)}) custom-call(bf16[256,1024]{1,0:T(8,128)(2,1)S(1)} %get-tuple-element.21.h, bf16[256,3072]{1,0:T(8,128)(2,1)S(1)} %get-tuple-element.22.s, bf16[1024,3072]{1,0:T(8,128)(2,1)S(1)} %get-tuple-element.23.w, f32[1024,3072]{1,0:T(8,128)S(1)} %get-tuple-element.24.t), custom_call_target="tpu_custom_call" | custom-call | flops 1610612736 | bytes 37748736 | tf_op jit(solution)/shard_map/update_out/pallas_call | solution.py:346
  71.8 5.7 %collective-permute-done.other = bf16[256,1024]{1,0:T(8,128)(2,1)S(1)} collective-permute-done((bf16[256,1024]{1,0:T(8,128)(2,1)S(1)}, bf16[256,1024]{1,0:T(8,128)(2,1)S(1)}, u32[]{:S(2)}, u32[]{:S(2)}) %collective-permute-start) | collective-permute-done | bytes 524320 | tf_op jit(solution)/shard_map/ppermute | solution.py:376
  77.5 0.0 slice-done
  77.5 0.0 slice-done.1
  77.5 0.0 slice-done.2
  77.5 7.3 %update_in.1 = (bf16[3072,1024]{1,0:T(8,128)(2,1)}, f32[3072,1024]{1,0:T(8,128)}) custom-call(bf16[256,3072]{1,0:T(8,128)(2,1)S(1)} %get-tuple-element.16.g, bf16[256,1024]{1,0:T(8,128)(2,1)S(1)} %get-tuple-element.17.part, bf16[256,1024]{1,0:T(8,128)(2,1)S(1)} %collective-permute-done.other, f32[256,1024]{1,0:T(8,128)S(1)} %get-tuple-element.18.gs, ...), custom_call_target="tpu_custom_call" | custom-call | flops 1610612736 | bytes 37748736 | tf_op jit(solution)/shard_map/update_in/pallas_call | solution.py:346
  (1 shorter events, 0.0 us)
Async XLA Ops:
  0.6 76.9 %slice-start = ((s8[12582912]{0:T(1024)(128)(4,1)}), s8[4194304]{0:T(1024)(128)(4,1)S(1)}, s32[]{:S(2)}) async-start(s8[12582912]{0:T(1024)(128)(4,1)} %bitcast), calls=%async_computation | async-start | bytes 8388608
  0.6 76.9 %slice-start.1 = ((s8[12582912]{0:T(1024)(128)(4,1)}), s8[4194304]{0:T(1024)(128)(4,1)S(1)}, s32[]{:S(2)}) async-start(s8[12582912]{0:T(1024)(128)(4,1)} %bitcast), calls=%async_computation.1 | async-start | bytes 8388608
  63.0 14.5 %collective-permute-start = (bf16[256,1024]{1,0:T(8,128)(2,1)S(1)}, bf16[256,1024]{1,0:T(8,128)(2,1)S(1)}, u32[]{:S(2)}, u32[]{:S(2)}) collective-permute-start(bf16[256,1024]{1,0:T(8,128)(2,1)S(1)} %get-tuple-element.17.part), channel_id=1, source_target_pairs={{0,1},{1,0},{2,3},{3,2},{4,5},{5,4},{6,7},{7,6},{8,9},{9,8},{10,11... | collective-permute-start | bytes 1572872 | tf_op jit(solution)/shard_map/ppermute | solution.py:376
  64.6 13.0 %slice-start.2 = ((s8[12582912]{0:T(1024)(128)(4,1)}), s8[4194304]{0:T(1024)(128)(4,1)S(1)}, s32[]{:S(2)}) async-start(s8[12582912]{0:T(1024)(128)(4,1)} %bitcast), calls=%async_computation.2 | async-start | bytes 8388608

commit v4 on v3

--- a/solution.py
+++ b/solution.py
@@ -31,13 +31,13 @@
 def forward_kernel(
     nz, in_scale, out_scale,
     x_hbm, t_hbm, w_in_hbm, w_out_hbm, teach_out_hbm,
-    g, h, s, part, pre, w_in, w_out, teach_out,
+    g, h, s, near, near_in, far, pre, w_in, w_out, teach_out,
     t_own, pre_send, pre_recv, acc, own,
     c_out, c_in, x_out, x_in, z_out, z_in,
     w_sem,
     ag_recv, ag_zs, ag_xs, ag_cs,
     sg_recv, sg_zs, sg_xs, sg_cs,
-    y_s, y_r, c_s, c_r, x_s, x_r, z_s, z_r,
+    y_s, y_r, c_s, c_r, x_s, x_r, z_s, z_r, n_s, n_r,
 ):
     rows, feats = t_own.shape
     ff = w_in.shape[1]
@@ -216,24 +216,36 @@
     s[mine, :] = slope.astype(BF16)
     begin()
 
+    half = 2 * group
+    tile = min(512, ff)
+
+    def slope_step(j, out):
+        at = pl.ds(pl.multiple_of((z_of(2 * j) // 2) * half, half), half)
+
+        @pl.loop(0, ff // tile)
+        def _(i):
+            units = pl.ds(pl.multiple_of(i * tile, tile), tile)
+            value = lax.dot_general(
+                s[at, :], w_out[units, :], (((1,), (1,)), ((), ())), preferred_element_type=F32
+            )
+            out[:, units] = (value * out_scale).astype(BF16)
+
     z_arrive(1)
     x_arrive(0)
     x_arrive(1)
+    c_arrive(0)
+    c_arrive(1)
+    slope_step(0, near)
+    swap = send(near, near_in, n_s.at[0], n_r.at[0], {"mp": 1 - my})
+    go(swap)
     for k in range(2, nz):
         z_arrive(k)
     for k in range(2, nz):
         x_arrive(k)
-    for k in range(nz):
+    for k in range(2, nz):
         c_arrive(k)
-    tile = min(512, ff)
-
-    @pl.loop(0, ff // tile)
-    def _(i):
-        units = pl.ds(pl.multiple_of(i * tile, tile), tile)
-        value = lax.dot_general(
-            s[...], w_out[units, :], (((1,), (1,)), ((), ())), preferred_element_type=F32
-        )
-        part[:, units] = (value * out_scale).astype(BF16)
+    slope_step(1, far)
+    swap.wait_recv()
 
     for copy in pending:
         copy.wait_send()
@@ -253,14 +265,16 @@
             pltpu.VMEM((tokens, feats), BF16),
             pltpu.VMEM((tokens, ff), BF16),
             pltpu.VMEM((tokens, feats), BF16),
-            pltpu.VMEM((tokens, ff), BF16),
+            pltpu.VMEM((tokens // 2, ff), BF16),
+            pltpu.VMEM((tokens // 2, ff), BF16),
+            pltpu.VMEM((tokens // 2, ff), BF16),
             pltpu.VMEM((tokens, ff), F32),
             pltpu.VMEM((feats, ff), BF16),
             pltpu.VMEM((ff, feats), BF16),
             pltpu.VMEM((ff, feats), F32),
         ),
         in_specs=[pl.BlockSpec(memory_space=pltpu.HBM)] * 5,
-        out_specs=(vmem,) * 8,
+        out_specs=(vmem,) * 10,
         scratch_shapes=[
             pltpu.VMEM((rows, feats), BF16),
             pltpu.VMEM((tokens, ff), BF16),
@@ -278,6 +292,7 @@
             dma((4 * nz,)), dma((nz,)), dma((nz,)), dma((2 * nz,)),
             dma((nz,)), dma((nz,)),
             dma((nz,)), dma((nz,)), dma((nz,)), dma((nz,)), dma((nz,)), dma((nz,)),
+            dma((1,)), dma((1,)),
         ],
         compiler_params=pltpu.CompilerParams(
             collective_id=0, has_side_effects=True, vmem_limit_bytes=12 * MIB
@@ -332,9 +347,13 @@
     write_update(scale, tile, cols, h, s, w, t, *rest)
 
 
-def in_kernel(scale, tile, cols, g, part, other, gs, w, t, grad_hbm, new_hbm, grads, news, turned, sems, pre_slope):
-    total = part[...].astype(F32) + other[...].astype(F32)
-    pre_slope[...] = (total * gs[...]).astype(BF16)
+def in_kernel(scale, tile, cols, g, near, near_in, far, far_in, gs, w, t, grad_hbm, new_hbm, grads, news, turned, sems, pre_slope):
+    half = near.shape[0]
+    side = lax.axis_index("dp") // 8
+    for here, there, first in ((near, near_in, side), (far, far_in, 1 - side)):
+        at = pl.ds(pl.multiple_of(first * half, half), half)
+        total = here[...].astype(F32) + there[...].astype(F32)
+        pre_slope[at, :] = (total * gs[at, :]).astype(BF16)
     write_update(scale, tile, cols, g, pre_slope, w, t, grad_hbm, new_hbm, grads, news, turned, sems)
 
 
@@ -370,17 +389,17 @@
     in_scale = 1.0 / math.sqrt(inputs.shape[1] * mp)
     out_scale = 1.0 / math.sqrt(w_out.shape[0] * dp)
     tokens, ff = inputs.shape[0] * dp, w_in.shape[1]
-    g, h, s, part, gs, w_in, w_out, teach_out = forward(
+    g, h, s, near, near_in, far, gs, w_in, w_out, teach_out = forward(
         dp // 4, in_scale, out_scale, inputs, targets, w_in, w_out, teach_out
     )
-    other = lax.ppermute(part, "mp", [(0, 1), (1, 0)])
+    far_in = lax.ppermute(far, "mp", [(0, 1), (1, 0)])
     grad_out, new_out = update(
         out_kernel, "update_out", out_scale, 128, 256, (), tokens,
         h, s, w_out, teach_out,
     )
     grad_in, new_in = update(
         in_kernel, "update_in", in_scale, 384, 256, (pltpu.VMEM((tokens, ff), BF16),), tokens,
-        g, part, other, gs, w_in, teach_in,
+        g, near, near_in, far, far_in, gs, w_in, teach_in,
     )
     return grad_in, grad_out, new_in, new_out
 

time: 85.9 us -> 84.2 us (0.980)
  waiting for transfers between devices: 5.7 us -> 0.01 us
  Pallas kernels: 76.9 us -> 80.7 us
    ppermute x1, waiting for transfers between devices: 5.7 us -> 0.01 us  [shards(): far_in = lax.ppermute(far, 'mp', [(0, 1), (1, 0)])]
    pallas_call x1, Pallas kernels: 62.3 us -> 66.1 us  [forward(): pl.pallas_call(functools.partial(forward_kernel, nz, in_scale, out_scale)...]
  transfers between devices with their start and end apart: 1 -> 1, of which waited for: 1 -> 0; matrix products, arithmetic and copies ran while one was open for 0% -> 0% of each run, Pallas kernels for 9% -> 9%
where the time goes in v4:
time: 84.2 us; the launch traced here: 83.8 us
  Pallas kernels  80.7 us (96%)
  starting transfers between devices  2.42 us (3%)
    pallas_call x1, Pallas kernels, forward(): pl.pallas_call(functools.partial(forward_kernel, nz, in_scale, out_scale)...  66.1 us
    pallas_call x2, Pallas kernels, update(): pl.pallas_call(functools.partial(kernel, scale, tile, cols), out_shape=(j...  14.6 us
    ppermute x1, starting transfers between devices, shards(): far_in = lax.ppermute(far, 'mp', [(0, 1), (1, 0)])  2.42 us
  transfers between devices with their start and end apart: 1, of which 0 were waited for; matrix products, arithmetic and copies ran while one was open for 0% of the time, Pallas kernels for 9%

profile of v4, /device:TPU:0, one launch (start us, length us, event | category | flops | bytes accessed | tf_op | source)
XLA Modules:
  0.0 83.8 jit_solution(11926264952546985391)
XLA Ops:
  0.6 0.0 slice-start
  0.6 0.0 slice-start.1
  0.7 66.1 %forward.1 = (bf16[256,3072]{1,0:T(8,128)(2,1)S(1)}, bf16[256,1024]{1,0:T(8,128)(2,1)S(1)}, bf16[256,3072]{1,0:T(8,128)(2,1)S(1)}, bf16[128,1024]{1,0:T(8,128)(2...) custom-call(bf16[16,3072]{1,0:T(8,128)(2,1)} %x_hbm.1, ...), custom_call_target="tpu_custom_call" | custom-call | flops 4831838208 | bytes 37748736 | tf_op jit(solution)/shard_map/forward/pallas_call | solution.py:262
  66.8 2.4 %collective-permute-start = (bf16[128,1024]{1,0:T(8,128)(2,1)S(1)}, bf16[128,1024]{1,0:T(8,128)(2,1)S(1)}, u32[]{:S(2)}, u32[]{:S(2)}) collective-permute-start(bf16[128,1024]{1,0:T(8,128)(2,1)S(1)} %get-tuple-element.21.far), channel_id=1, source_target_pairs={{0,1},{1,0},{2,3},{3,2},{4,5},{5,4},{6,7},{7,6},{8,9},{9,8},{10,11... | collective-permute-start | bytes 786440 | tf_op jit(solution)/shard_map/ppermute | solution.py:395
  69.2 0.0 slice-start.2
  69.2 7.2 %update_out.1 = (bf16[1024,3072]{1,0:T(8,128)(2,1)}, f32[1024,3072]{1,0:T(8,128)}) custom-call(bf16[256,1024]{1,0:T(8,128)(2,1)S(1)} %get-tuple-element.25.h, bf16[256,3072]{1,0:T(8,128)(2,1)S(1)} %get-tuple-element.26.s, bf16[1024,3072]{1,0:T(8,128)(2,1)S(1)} %get-tuple-element.27.w, f32[1024,3072]{1,0:T(8,128)S(1)} %get-tuple-element.28.t), custom_call_target="tpu_custom_call" | custom-call | flops 1610612736 | bytes 37748736 | tf_op jit(solution)/shard_map/update_out/pallas_call | solution.py:365
  76.5 0.0 collective-permute-done.far_in
  76.5 0.0 slice-done
  76.5 0.0 slice-done.1
  76.5 0.0 slice-done.2
  76.5 7.3 %update_in.1 = (bf16[3072,1024]{1,0:T(8,128)(2,1)}, f32[3072,1024]{1,0:T(8,128)}) custom-call(bf16[256,3072]{1,0:T(8,128)(2,1)S(1)} %get-tuple-element.18.g, bf16[128,1024]{1,0:T(8,128)(2,1)S(1)} %get-tuple-element.19.near, bf16[128,1024]{1,0:T(8,128)(2,1)S(1)} %get-tuple-element.20.near_in, bf16[128,1024]{1,0:T(8,128)(2,1)S(1)} %get-tuple-element.21.far, ...), custom_call_target="tpu_custom_call" | custom-call | flops 1610612736 | bytes 37748736 | tf_op jit(solution)/shard_map/update_in/pallas_call | solution.py:365
  (1 shorter events, 0.0 us)
Async XLA Ops:
  0.6 75.9 %slice-start = ((s8[12582912]{0:T(1024)(128)(4,1)}), s8[4194304]{0:T(1024)(128)(4,1)S(1)}, s32[]{:S(2)}) async-start(s8[12582912]{0:T(1024)(128)(4,1)} %bitcast), calls=%async_computation | async-start | bytes 8388608
  0.6 75.9 %slice-start.1 = ((s8[12582912]{0:T(1024)(128)(4,1)}), s8[4194304]{0:T(1024)(128)(4,1)S(1)}, s32[]{:S(2)}) async-start(s8[12582912]{0:T(1024)(128)(4,1)} %bitcast), calls=%async_computation.1 | async-start | bytes 8388608
  66.8 9.7 %collective-permute-start = (bf16[128,1024]{1,0:T(8,128)(2,1)S(1)}, bf16[128,1024]{1,0:T(8,128)(2,1)S(1)}, u32[]{:S(2)}, u32[]{:S(2)}) collective-permute-start(bf16[128,1024]{1,0:T(8,128)(2,1)S(1)} %get-tuple-element.21.far), channel_id=1, source_target_pairs={{0,1},{1,0},{2,3},{3,2},{4,5},{5,4},{6,7},{7,6},{8,9},{9,8},{10,11... | collective-permute-start | bytes 786440 | tf_op jit(solution)/shard_map/ppermute | solution.py:395
  69.2 7.3 %slice-start.2 = ((s8[12582912]{0:T(1024)(128)(4,1)}), s8[4194304]{0:T(1024)(128)(4,1)S(1)}, s32[]{:S(2)}) async-start(s8[12582912]{0:T(1024)(128)(4,1)} %bitcast), calls=%async_computation.2 | async-start | bytes 8388608
